TPU v7x, 1024 devices: a whole 4x4x32 slice. The times are simulated.
1024 devices in a mesh: fsdp: 32 (over z_lo, core), rep: 32 (over x, y, z_hi).
Axes of the slice: x: 4, y: 4, z: 32 (z_hi: 2, z_lo: 16; z = z_hi * 16 + z_lo), core: 2. Of those that a mesh axis runs over, the one named last changes fastest.
Arguments:
- tokens: bfloat16 [196608, 4096], P(('fsdp', 'rep')), may hold values from -24 to 24
- frozen_base_weight: bfloat16 [4096, 512], P('fsdp'), may hold values from -8 to 8
- adapter_down_factor: bfloat16 [4096, 64], P('fsdp'), may hold values from -0.09375 to 0.09375
- adapter_up_factor: bfloat16 [64, 512], replicated, may hold values from -0.75 to 0.75
- magnitude: float32 [512], replicated, may hold values from 0.5 to 2
- output_cotangent: bfloat16 [196608, 512], P(('fsdp', 'rep')), may hold values from -8 to 8
Outputs:
- layer_out: bfloat16 [196608, 512], P(('fsdp', 'rep'))
- input_gradient: bfloat16 [196608, 4096], P(('fsdp', 'rep'))
- mag_grad: float32 [512], replicated
- up_grad: float32 [64, 512], replicated
- down_grad: float32 [4096, 64], P('fsdp')
All inputs are finite; a program needn't handle non-finite values.
Results may differ from a plain program's by a relative error of at most 0.0055.
Values may be sent and summed in bfloat16 or wider, within the bound.
A program may use at most 32 MiB of HBM per device.

v0:
```python
import math

import jax
import jax.numpy as jnp
from jax import lax
from jax.sharding import PartitionSpec as P


def body(
    tokens, frozen_base_weight, adapter_down_factor, adapter_up_factor, magnitude, output_cotangent
):
    whole_base, whole_down = (
        lax.all_gather(frozen_base_weight, "fsdp", axis=0, tiled=True),
        lax.all_gather(adapter_down_factor, "fsdp", axis=0, tiled=True),
    )
    merged_weight = frozen_base_weight.astype(jnp.float32) + 2.0 * jnp.dot(
        adapter_down_factor, adapter_up_factor, preferred_element_type=jnp.float32
    )
    squares = lax.psum(jnp.sum(merged_weight * merged_weight, axis=0), "fsdp")
    col_norm = jnp.sqrt(squares + 1e-06)
    scaling = magnitude / col_norm
    low_rank_update = jnp.dot(tokens, whole_down, preferred_element_type=jnp.float32).astype(
        jnp.bfloat16
    )
    linear_output = jnp.dot(tokens, whole_base, preferred_element_type=jnp.float32) + 2.0 * jnp.dot(
        low_rank_update, adapter_up_factor, preferred_element_type=jnp.float32
    )
    layer_out = (linear_output * scaling).astype(jnp.bfloat16)
    scaled_output = (output_cotangent.astype(jnp.float32) * scaling).astype(jnp.bfloat16)
    backward_low_rank = lax.dot_general(
        scaled_output,
        adapter_up_factor,
        (((1,), (1,)), ((), ())),
        preferred_element_type=jnp.float32,
    ).astype(jnp.bfloat16)
    input_gradient = lax.dot_general(
        scaled_output, whole_base, (((1,), (1,)), ((), ())), preferred_element_type=jnp.float32
    )
    input_gradient = (
        input_gradient
        + 2.0
        * lax.dot_general(
            backward_low_rank,
            whole_down,
            (((1,), (1,)), ((), ())),
            preferred_element_type=jnp.float32,
        )
    ).astype(jnp.bfloat16)
    overall = tokens.shape[0] * lax.axis_size("fsdp") * lax.axis_size("rep")
    factor = 1.0 / math.sqrt(overall)
    mag_term = (
        jnp.sum(output_cotangent.astype(jnp.float32) * linear_output, axis=0) / col_norm * factor
    )
    up_term = (
        2.0
        * factor
        * lax.dot_general(
            low_rank_update,
            scaled_output,
            (((0,), (0,)), ((), ())),
            preferred_element_type=jnp.float32,
        )
    )
    row_sums = lax.psum_scatter(
        2.0
        * factor
        * lax.dot_general(
            tokens, backward_low_rank, (((0,), (0,)), ((), ())), preferred_element_type=jnp.float32
        ),
        "fsdp",
        scatter_dimension=0,
        tiled=True,
    )
    up_grad, mag_grad = lax.psum((up_term, mag_term), ("fsdp", "rep"))
    down_grad = lax.psum(row_sums, "rep")
    return (layer_out, input_gradient, mag_grad, up_grad, down_grad)


def solution(mesh):
    placed = (
        P(("fsdp", "rep"), None),
        P("fsdp", None),
        P("fsdp", None),
        P(),
        P(),
        P(("fsdp", "rep"), None),
    )
    return jax.shard_map(
        body,
        mesh=mesh,
        in_specs=placed,
        out_specs=(P(("fsdp", "rep"), None), P(("fsdp", "rep"), None), P(), P(), P("fsdp", None)),
        check_vma=False,
    )
```

profile of v0, /device:TPU:1, one launch (start us, length us, event | category | flops | bytes accessed | tf_op | source)
XLA Modules:
  0.0 1176.9 jit_solution(7365006562029754484)
XLA Ops:
  8.0 0.0 copy-start
  8.0 0.0 copy-start.4
  8.0 0.0 reduce-scatter.2.cloned.1.call-start
  8.1 1.3 fusion.5
  9.4 179.6 %psum.28 = f32[512]{0:T(512)S(1)} all-reduce(f32[512]{0:T(512)S(1)} %fusion.5), channel_id=1, replica_groups=mesh['fsdp'=32,'rep'=32] {'fsdp'}, use_global_device_ids=true, to_apply=%region_1.0 | all-reduce | flops 512 | bytes 4096 | tf_op jit(solution)/shard_map/psum | solution.py:19
  189.0 0.7 fusion.11
  189.7 1.1 convolution_convert_fusion
  190.8 0.0 copy-done
  190.8 0.0 copy-start.2
  190.8 1.4 fusion.1
  192.2 0.0 reduce-scatter.2.cloned.1.call-update
  192.2 0.0 all-gather.2.cloned.1.call-start
  192.3 0.7 all-gather.2.cloned.1.call-update
  193.0 0.0 all-reduce.2.cloned.1.call-start
  193.0 0.0 copy-done.4
  193.0 101.1 %all_gather.7 = bf16[4096,64]{0,1:T(8,128)(2,1)S(1)} all-gather(bf16[128,64]{0,1:T(8,128)(2,1)S(1)} %copy-done.4), channel_id=1, replica_groups=mesh['fsdp'=32,'rep'=32] {'fsdp'}, dimensions={0}, use_global_device_ids=true | all-gather | bytes 540672 | tf_op jit(solution)/shard_map/all_gather | solution.py:14
  294.2 0.7 convolution_convert_fusion.1
  294.8 0.0 copy-done.2
  294.8 0.8 convolution_multiply_fusion.4
  295.7 0.0 all-reduce.2.cloned.1.call-update
  295.7 2.3 convolution_multiply_fusion
  298.0 0.0 copy-start.3
  298.0 238.3 %reduce-scatter.2.cloned.1.call-done = f32[128,64]{0,1:T(8,128)} async-done(((f32[4096,64]{0,1:T(8,128)}), f32[128,64]{0,1:T(8,128)}) %reduce-scatter.2.cloned.1.call-update) | async-done | bytes 32784 | tf_op jit(solution)/shard_map/reduce_scatter | solution.py:64
  536.3 442.5 %psum.31 = f32[128,64]{0,1:T(8,128)} all-reduce(f32[128,64]{0,1:T(8,128)} %reduce-scatter.2.cloned.1.call-done), channel_id=1, replica_groups=mesh['fsdp'=32,'rep'=32] {'rep'}, use_global_device_ids=true, to_apply=%region_6.0 | all-reduce | flops 8192 | bytes 65536 | tf_op jit(solution)/shard_map/psum | solution.py:75
  978.8 0.0 all-gather.2.cloned.1.call-done
  978.8 0.0 copy-start.1
  978.8 3.3 fusion.12
  982.1 0.0 copy-done.3
  982.2 0.9 fusion.7
  983.1 0.0 copy-done.1
  983.1 4.6 fusion
  987.7 180.2 %psum.29 = f32[512]{0:T(512)} all-reduce(f32[512]{0:T(512)S(1)} %divide_multiply_fusion), channel_id=1, replica_groups=mesh['fsdp'=32,'rep'=32] {'fsdp','rep'}, use_global_device_ids=true, to_apply=%region_3.0 | all-reduce | flops 512 | bytes 4096 | tf_op jit(solution)/shard_map/psum | solution.py:74
  1167.9 0.0 all-reduce.2.cloned.1.call-done
  1167.9 1.6 copy.12
  (1 shorter events, 0.0 us)
Async XLA Ops:
  8.0 182.8 %copy-start = (bf16[192,4096]{1,0:T(8,128)(2,1)S(1)}, bf16[192,4096]{1,0:T(8,128)(2,1)}, u32[]{:S(2)}) copy-start(bf16[192,4096]{1,0:T(8,128)(2,1)} %param.6) | copy-start | bytes 4718596
  8.0 185.0 %copy-start.4 = (bf16[128,64]{0,1:T(8,128)(2,1)S(1)}, bf16[128,64]{0,1:T(8,128)(2,1)}, u32[]{:S(2)}) copy-start(bf16[128,64]{0,1:T(8,128)(2,1)} %param.8) | copy-start | bytes 49156
  8.0 528.3 %reduce-scatter.2.cloned.1.call-start = ((), (), s32[]{:S(2)}) async-start(), calls=%async_computation.3 | async-start | bytes 1081344 | tf_op jit(solution)/shard_map/reduce_scatter | solution.py:64
  190.8 104.0 %copy-start.2 = (bf16[192,512]{1,0:T(8,128)(2,1)S(1)}, bf16[192,512]{1,0:T(8,128)(2,1)}, u32[]{:S(2)}) copy-start(bf16[192,512]{1,0:T(8,128)(2,1)} %param.11) | copy-start | bytes 589828
  192.2 786.6 %all-gather.2.cloned.1.call-start = ((), (), s32[]{:S(2)}) async-start(), calls=%async_computation.1 | async-start | bytes 4325376 | tf_op jit(solution)/shard_map/all_gather | solution.py:13
  193.0 974.9 %all-reduce.2.cloned.1.call-start = ((), (), s32[]{:S(2)}) async-start(), calls=%async_computation.2 | async-start | bytes 262144 | tf_op jit(solution)/shard_map/psum | solution.py:74
  298.0 684.2 %copy-start.3 = (bf16[64,512]{1,0:T(8,128)(2,1)S(1)}, bf16[64,512]{1,0:T(8,128)(2,1)}, u32[]{:S(2)}) copy-start(bf16[64,512]{1,0:T(8,128)(2,1)} %param.9) | copy-start | bytes 196612
  978.8 4.3 copy-start.1
Sparse Core Ops, SparseCore 0:
  192.4 343.8 reduce-scatter.1
  539.3 335.4 all-gather.1
Sparse Core Ops, SparseCore 1:
  295.8 843.8 all-reduce.1
where the time goes:
time: 1180 us
  blocking collectives  904 us (77%)
  waiting for transfers between devices  239 us (20%)
  matrix products  16.4 us (1%)
  between operations  15.6 us (1%)
    psum x1, blocking collectives, body(): down_grad = lax.psum(row_sums, 'rep')  443 us
    reduce_scatter x1, waiting for transfers between devices, body(): lax.psum_scatter(2.0 * factor * lax.dot_general(tokens, backward_low_rank...  238 us
    psum x1, blocking collectives, body(): up_grad, mag_grad = lax.psum((up_term, mag_term), ('fsdp', 'rep'))  180 us
    psum x1, blocking collectives, body(): squares = lax.psum(jnp.sum(merged_weight * merged_weight, axis=0), 'fsdp')  180 us
    all_gather x1, blocking collectives, body(): lax.all_gather(adapter_down_factor, 'fsdp', axis=0, tiled=True)  101 us
  transfers between devices with their start and end apart: 3, of which 1 were waited for; matrix products, arithmetic and copies ran while one was open for 1% of the time, Pallas kernels for 0%

commit v1 on v0

v1 whole, which is shorter than its diff:
```python
import math

import jax
import jax.numpy as jnp
from jax import lax
from jax.experimental import pallas as pl
from jax.experimental.pallas import tpu as pltpu
from jax.sharding import PartitionSpec as P

MESH = pl.DeviceIdType.MESH
F32, BF16 = jnp.float32, jnp.bfloat16
TOK, FEAT, UNITS, RANK = 192, 4096, 512, 64
NT = (((1,), (1,)), ((), ()))
TN = (((0,), (0,)), ((), ()))


class Slots:
    def __init__(self):
        self.used = 0

    def take(self, count):
        base = self.used
        self.used += count
        return base


SLOTS = Slots()
LOCAL = SLOTS.take(6)
N_CORE = SLOTS.take(1)
N_Z = SLOTS.take(16)
A_Z = SLOTS.take(16)
A_X = SLOTS.take(4)
A_CORE = SLOTS.take(1)
W_RIGHT = SLOTS.take(16)
W_LEFT = SLOTS.take(16)
W_CORE = SLOTS.take(16)
D_CORE = SLOTS.take(1)
D_X = SLOTS.take(4)
D_Y = SLOTS.take(4)
D_Q = SLOTS.take(4)
D_O = SLOTS.take(8)
D_P = SLOTS.take(16)
U_CORE = SLOTS.take(1)
U_X = SLOTS.take(4)
U_Y = SLOTS.take(4)
U_Q = SLOTS.take(4)
U_O = SLOTS.take(8)
U_P = SLOTS.take(16)
U_PC = SLOTS.take(1)
M_CORE = SLOTS.take(1)
M_P = SLOTS.take(16)
M_Q = SLOTS.take(4)
M_O = SLOTS.take(8)
OUT = SLOTS.take(18)
TOTAL = SLOTS.used

Z_OFFSETS = tuple(d for d in range(-7, 9) if d)


def device(x, y, z, c):
    x, y, z = lax.rem(x + 4, 4), lax.rem(y + 4, 4), lax.rem(z + 32, 32)
    return {"fsdp": lax.rem(z, 16) * 2 + c, "rep": (x * 4 + y) * 2 + z // 16}


def kernel(
    tok_hbm, base_hbm, down_hbm, up_hbm, mag_hbm, cot_hbm,
    lay_hbm, inp_hbm, mg_ref, ug_ref, dg_ref,
    tok, own_a, b_ref, mag, cot,
    wg, apk, ap, af,
    n_core, n_z,
    scaled_ref, back_ref, lin, lay, inp,
    d_all, d_core, d_x, d_y, d_f, d_q, d_g, d_o, d_h, d_p,
    u_all, u_core, u_e, u_x, u_f, u_y, u_g, u_q, u_h, u_o, u_p,
    m_core, m_p, m_q, m_o, m_g, m_h,
    ss, rs,
):
    f_at, r_at = lax.axis_index("fsdp"), lax.axis_index("rep")
    c, zl = lax.rem(f_at, 2), f_at // 2
    zh, xy = lax.rem(r_at, 2), r_at // 2
    x, y, z = xy // 4, lax.rem(xy, 4), zh * 16 + zl
    qb, qa = lax.rem(z, 4), z // 4
    sib = device(x, y, z, 1 - c)
    overall = 196608.0
    factor = 1.0 / math.sqrt(overall)

    def remote(src, dst, s, r, to):
        return pltpu.make_async_remote_copy(
            src_ref=src, dst_ref=dst, send_sem=ss.at[s], recv_sem=rs.at[r],
            device_id=to, device_id_type=MESH,
        )

    def arrived(dst, r):
        remote(dst, dst, r, r, sib).wait_recv()

    def left_here(src, s):
        remote(src, src, s, s, sib).wait_send()

    rows_c = pl.ds(pl.multiple_of(c * 128, 128), 128)
    loads = [
        pltpu.make_async_copy(base_hbm, wg.at[zl, rows_c], rs.at[LOCAL]),
        pltpu.make_async_copy(down_hbm, own_a, rs.at[LOCAL + 1]),
        pltpu.make_async_copy(up_hbm, b_ref, rs.at[LOCAL + 2]),
        pltpu.make_async_copy(mag_hbm, mag, rs.at[LOCAL + 3]),
        pltpu.make_async_copy(cot_hbm, cot, rs.at[LOCAL + 4]),
        pltpu.make_async_copy(tok_hbm, tok, rs.at[LOCAL + 5]),
    ]
    for load in loads:
        load.start()

    barrier = pltpu.get_barrier_semaphore()
    peers = [sib]
    peers += [device(x + i, y + j, z, c) for i in range(4) for j in range(4) if i or j]
    peers += [device(x, y, z + d, c) for d in (*range(-8, 0), *range(1, 9), 12, -12, 16)]
    for peer in peers:
        pl.semaphore_signal(barrier, 1, device_id=peer, device_id_type=MESH)

    loads[0].wait()
    loads[1].wait()
    loads[2].wait()
    w_own = wg[zl, rows_c].astype(F32)
    merged = w_own + 2.0 * jnp.dot(own_a[...], b_ref[...], preferred_element_type=F32)
    n_core[c] = jnp.sum(merged * merged, axis=0, keepdims=True)
    apk[...] = jnp.concatenate([own_a[0:64, :], own_a[64:128, :]], axis=1)
    ap[c, x, zl] = apk[pl.ds(pl.multiple_of(x * 16, 16), 16), :]
    pl.semaphore_wait(barrier, len(peers))

    right, left = device(x, y, z + 1, c), device(x, y, z - 1, c)

    n_copy = remote(n_core.at[c], n_core.at[c], N_CORE, N_CORE, sib)
    n_copy.start()

    def half(res, h):
        return wg.at[res, pl.ds(pl.multiple_of(c * 128 + h * 64, 64), 64)]

    def ring_copy(to_right, k, h):
        res = lax.rem(zl - k + 16, 16) if to_right else lax.rem(zl + k, 16)
        at = (W_RIGHT if to_right else W_LEFT) + k * 2 + h
        return remote(half(res, h), half(res, h), at, at, right if to_right else left)

    def active(to_right, k):
        if k < 7:
            return (0, 1)
        return (0,) if to_right else (1,)

    def w_core(res):
        part = wg.at[res, rows_c]
        return remote(part, part, W_CORE + res, W_CORE + res, sib)

    for h in (0, 1):
        ring_copy(True, 0, h).start()
        ring_copy(False, 0, h).start()
    w_core(zl).start()

    def a_send(i, _):
        d = i - 7

        @pl.when(d != 0)
        def _():
            remote(
                ap.at[c, x, zl], ap.at[c, x, zl], A_Z + i, A_Z + zl, device(x, y, z + d, c)
            ).start()

        return 0

    lax.fori_loop(0, 16, a_send, 0)

    n_copy.wait()
    n_z[zl] = n_core[0] + n_core[1]

    def n_send(i, _):
        d = i - 7

        @pl.when(d != 0)
        def _():
            remote(n_z.at[zl], n_z.at[zl], N_Z + i, N_Z + zl, device(x, y, z + d, c)).start()

        return 0

    lax.fori_loop(0, 16, n_send, 0)

    def ring_step(k):
        for h in (0, 1):
            for to_right in (True, False):
                if h in active(to_right, k):
                    res = lax.rem(zl - 1 - k + 16, 16) if to_right else lax.rem(zl + 1 + k, 16)
                    at = (W_RIGHT if to_right else W_LEFT) + k * 2 + h
                    arrived(half(res, h), at)
                    if k < 7 and h in active(to_right, k + 1):
                        ring_copy(to_right, k + 1, h).start()
        if k < 7:
            w_core(lax.rem(zl - 1 - k + 16, 16)).start()
            w_core(lax.rem(zl + 1 + k, 16)).start()
        else:
            w_core(lax.rem(zl + 8, 16)).start()

    ring_step(0)

    def n_wait(i, _):
        d = i - 7

        @pl.when(d != 0)
        def _():
            slot = lax.rem(zl - d + 16, 16)
            arrived(n_z.at[slot], N_Z + slot)

        return 0

    lax.fori_loop(0, 16, n_wait, 0)
    loads[3].wait()
    loads[4].wait()
    squares = jnp.sum(n_z[...], axis=0)
    col_norm = jnp.sqrt(squares + 1e-06)
    scaling = mag[...] / col_norm
    scaled = (cot[...].astype(F32) * scaling).astype(BF16)
    scaled_ref[...] = scaled
    back = lax.dot_general(scaled, b_ref[...], NT, preferred_element_type=F32).astype(BF16)
    back_ref[...] = back
    loads[5].wait()

    def columns(res):
        return pl.ds(pl.multiple_of(res * 256, 256), 256)

    def d_part(res, _):
        part = (2.0 * factor) * lax.dot_general(
            back_ref[...], tok[:, columns(res)], TN, preferred_element_type=F32
        )
        for k in range(2):
            d_all[k, :, res] = part[:, k * 128 : k * 128 + 128].reshape(4, 16, 128)
        return 0

    lax.fori_loop(0, 16, d_part, 0)
    d_core_copy = remote(d_all.at[1 - c], d_core, D_CORE, D_CORE, sib)
    d_core_copy.start()
    ring_step(1)

    def a_wait(i, _):
        d = i - 7

        @pl.when(d != 0)
        def _():
            slot = lax.rem(zl - d + 16, 16)
            arrived(ap.at[c, x, slot], A_Z + slot)

        return 0

    lax.fori_loop(0, 16, a_wait, 0)
    for d in (1, 2, 3):
        remote(ap.at[c, x], ap.at[c, x], A_X + d, A_X + d, device(x + d, y, z, c)).start()

    d_core_copy.wait()

    def d_sum(i, _):
        d_core[i] = d_core[i] + d_all[c, i]
        return 0

    lax.fori_loop(0, 4, d_sum, 0)
    for d in (1, 2, 3):
        remote(
            d_core.at[lax.rem(x + d, 4)], d_x.at[x], D_X + d, D_X + d, device(x + d, y, z, c)
        ).start()
    ring_step(2)

    for d in (1, 2, 3):
        xs = lax.rem(x - d + 4, 4)
        arrived(ap.at[c, xs], A_X + d)
    a_core_copy = remote(ap.at[c], ap.at[c], A_CORE, A_CORE, sib)
    a_core_copy.start()
    ring_step(3)
    arrived(ap.at[1 - c], A_CORE)
    for k in range(2):
        for q in range(4):
            part = ap[k, q]
            af[:, k, 0, q] = part[:, :, 0:64]
            af[:, k, 1, q] = part[:, :, 64:128]
    low = jnp.dot(tok[...], af[...].reshape(FEAT, RANK), preferred_element_type=F32).astype(BF16)
    up_part = (2.0 * factor) * lax.dot_general(low, scaled_ref[...], TN, preferred_element_type=F32)
    for k in range(2):
        for q in range(4):
            u_all[k, q] = up_part[k * 32 : k * 32 + 32, q * 128 : q * 128 + 128]
    lin[...] = 2.0 * jnp.dot(low, b_ref[...], preferred_element_type=F32)
    u_core_copy = remote(u_all.at[1 - c], u_core, U_CORE, U_CORE, sib)
    u_core_copy.start()

    d_x[x] = d_core[x]
    for d in (1, 2, 3):
        arrived(d_x.at[lax.rem(x - d + 4, 4)], D_X + d)
    d_f[...] = ((d_x[0] + d_x[1]) + (d_x[2] + d_x[3])).reshape(4, 4, 16, 128)
    for d in (1, 2, 3):
        remote(
            d_f.at[lax.rem(y + d, 4)], d_y.at[y], D_Y + d, D_Y + d, device(x, y + d, z, c)
        ).start()
    u_core_copy.wait()
    u_e[...] = u_all[c] + u_core[...]
    for d in (1, 2, 3):
        remote(
            u_e.at[lax.rem(x + d, 4)], u_x.at[x], U_X + d, U_X + d, device(x + d, y, z, c)
        ).start()
    ring_step(4)

    def consume(res):
        w_pair = wg[res]
        a_pair = af[res].reshape(256, RANK)
        lin[...] += jnp.dot(tok[:, columns(res)], w_pair, preferred_element_type=F32)
        grad = lax.dot_general(scaled_ref[...], w_pair, NT, preferred_element_type=F32)
        grad = grad + 2.0 * lax.dot_general(
            back_ref[...], a_pair, NT, preferred_element_type=F32
        )
        inp[:, columns(res)] = grad.astype(BF16)
        pltpu.make_async_copy(
            inp.at[:, columns(res)], inp_hbm.at[:, columns(res)], rs.at[OUT + res]
        ).start()

    def consume_range(first, last):
        def one(j, _):
            res = lax.rem(zl + j + (first + 16), 16)
            arrived(wg.at[res, pl.ds(pl.multiple_of((1 - c) * 128, 128), 128)], W_CORE + res)
            consume(res)
            return 0

        lax.fori_loop(0, last - first, one, 0)

    consume_range(-3, 4)

    d_y[y] = d_f[y]
    for d in (1, 2, 3):
        arrived(d_y.at[lax.rem(y - d + 4, 4)], D_Y + d)
    d_g[...] = (d_y[0] + d_y[1]) + (d_y[2] + d_y[3])
    for d in (1, 2, 3):
        to = lax.rem(qb + d, 4)
        remote(d_g.at[to], d_q.at[qb], D_Q + d, D_Q + d, device(x, y, qa * 4 + to, c)).start()
    u_x[x] = u_e[x]
    for d in (1, 2, 3):
        arrived(u_x.at[lax.rem(x - d + 4, 4)], U_X + d)
    u_f[...] = ((u_x[0] + u_x[1]) + (u_x[2] + u_x[3])).reshape(4, 8, 128)
    for d in (1, 2, 3):
        remote(
            u_f.at[lax.rem(y + d, 4)], u_y.at[y], U_Y + d, U_Y + d, device(x, y + d, z, c)
        ).start()
    ring_step(5)

    owner = lax.rem(qa, 4) == y
    d_q[qb] = d_g[qb]
    for d in (1, 2, 3):
        arrived(d_q.at[lax.rem(qb - d + 4, 4)], D_Q + d)
    d_h[...] = (d_q[0] + d_q[1]) + (d_q[2] + d_q[3])
    for hi in (0, 1):
        to = y + 4 * hi

        @pl.when(to != qa)
        def _():
            remote(d_h, d_o.at[qa], D_O + hi, D_O + qa, device(x, y, to * 4 + qb, c)).start()

    u_y[y] = u_f[y]
    for d in (1, 2, 3):
        arrived(u_y.at[lax.rem(y - d + 4, 4)], U_Y + d)
    u_q[qb] = (u_y[0] + u_y[1]) + (u_y[2] + u_y[3])
    for d in (1, 2, 3):
        to = lax.rem(qb + d, 4)
        remote(u_q.at[qb], u_q.at[qb], U_Q + d, U_Q + d, device(x, y, qa * 4 + to, c)).start()
    ring_step(6)
    for d in (1, 2, 3):
        arrived(u_q.at[lax.rem(qb - d + 4, 4)], U_Q + d)
    u_o[qa] = (u_q[0] + u_q[1]) + (u_q[2] + u_q[3])
    for d in range(1, 8):
        to = lax.rem(qa + d, 8)
        remote(u_o.at[qa], u_o.at[qa], U_O + d, U_O + d, device(x, y, to * 4 + qb, c)).start()
    ring_step(7)
    consume_range(4, 13)

    linear = lin[...]
    lay[...] = (linear * scaling).astype(BF16)
    lay_copy = pltpu.make_async_copy(lay, lay_hbm, rs.at[OUT + 16])
    lay_copy.start()
    m_core[c] = jnp.sum(cot[...].astype(F32) * linear, axis=0, keepdims=True)
    m_core_copy = remote(m_core.at[c], m_core.at[c], M_CORE, M_CORE, sib)
    m_core_copy.start()
    m_core_copy.wait()
    m_p[xy] = m_core[0] + m_core[1]

    def plane(i):
        return lax.rem(xy // 4 + i // 4, 4), lax.rem(lax.rem(xy, 4) + lax.rem(i, 4), 4)

    def m_send(i, _):
        px, py = plane(i)
        remote(m_p.at[xy], m_p.at[xy], M_P + i, M_P + xy, device(px, py, z, c)).start()
        return 0

    lax.fori_loop(1, 16, m_send, 0)

    @pl.when(owner)
    def _():
        d_o[qa] = d_h[...]
        for d in range(1, 8):
            at = lax.rem(qa - d + 8, 8)
            arrived(d_o.at[at], D_O + at)
        total = ((d_o[0] + d_o[1]) + (d_o[2] + d_o[3])) + ((d_o[4] + d_o[5]) + (d_o[6] + d_o[7]))
        d_p[x] = total

        def d_send(i, _):
            px, py = plane(i)
            remote(d_p.at[x], d_p.at[x], D_P + i, D_P + x, device(px, py, z, c)).start()
            return 0

        lax.fori_loop(1, 16, d_send, 0)

    for d in range(1, 8):
        arrived(u_o.at[lax.rem(qa - d + 8, 8)], U_O + d)
    u_p[c, xy] = ((u_o[0] + u_o[1]) + (u_o[2] + u_o[3])) + ((u_o[4] + u_o[5]) + (u_o[6] + u_o[7]))

    def u_send(i, _):
        px, py = plane(i)
        remote(u_p.at[c, xy], u_p.at[c, xy], U_P + i, U_P + xy, device(px, py, z, c)).start()
        return 0

    lax.fori_loop(1, 16, u_send, 0)

    def m_wait(i, _):
        px, py = plane(i)
        slot = px * 4 + py
        arrived(m_p.at[slot], M_P + slot)
        return 0

    lax.fori_loop(1, 16, m_wait, 0)
    m_q[qb] = jnp.sum(m_p[...], axis=0)
    for d in (1, 2, 3):
        to = lax.rem(qb + d, 4)
        remote(m_q.at[qb], m_q.at[qb], M_Q + d, M_Q + d, device(x, y, qa * 4 + to, c)).start()

    for d in (1, 2, 3):
        arrived(m_q.at[lax.rem(qb - d + 4, 4)], M_Q + d)
    m_o[qa] = (m_q[0] + m_q[1]) + (m_q[2] + m_q[3])
    for d in range(1, 8):
        to = lax.rem(qa + d, 8)
        remote(m_o.at[qa], m_o.at[qa], M_O + d, M_O + d, device(x, y, to * 4 + qb, c)).start()

    def u_wait(i, _):
        px, py = plane(i)
        slot = px * 4 + py
        arrived(u_p.at[c, slot], U_P + slot)
        return 0

    lax.fori_loop(1, 16, u_wait, 0)
    u_pc = remote(u_p.at[c], u_p.at[c], U_PC, U_PC, sib)
    u_pc.start()

    def d_wait(s, _):
        @pl.when(jnp.logical_or(s != x, jnp.logical_not(owner)))
        def _():
            arrived(d_p.at[s], D_P + s)

        return 0

    lax.fori_loop(0, 4, d_wait, 0)
    dg_ref[...] = d_p[...].reshape(64, 128).T
    arrived(u_p.at[1 - c], U_PC)
    for k in range(2):
        for q in range(4):
            ug_ref[k * 32 : k * 32 + 32, q * 128 : q * 128 + 128] = u_p[
                k, q * 4 : q * 4 + 4
            ].reshape(32, 128)
    for d in range(1, 8):
        arrived(m_o.at[lax.rem(qa - d + 8, 8)], M_O + d)
    m_sum = ((m_o[0] + m_o[1]) + (m_o[2] + m_o[3])) + ((m_o[4] + m_o[5]) + (m_o[6] + m_o[7]))
    mg_ref[...] = m_sum / col_norm * factor

    def sent_z(i, _):
        @pl.when(i != 7)
        def _():
            left_here(ap.at[c, x, zl], A_Z + i)
            left_here(n_z.at[zl], N_Z + i)

        @pl.when(i != 0)
        def _():
            left_here(m_p.at[xy], M_P + i)
            left_here(u_p.at[c, xy], U_P + i)

            @pl.when(owner)
            def _():
                left_here(d_p.at[x], D_P + i)

        left_here(wg.at[i, rows_c], W_CORE + i)
        pltpu.make_async_copy(
            inp.at[:, columns(i)], inp_hbm.at[:, columns(i)], rs.at[OUT + i]
        ).wait()
        return 0

    lax.fori_loop(0, 16, sent_z, 0)
    for k in range(8):
        for to_right in (True, False):
            for h in active(to_right, k):
                ring_copy(to_right, k, h).wait_send()
    for d in (1, 2, 3):
        left_here(ap.at[c, x], A_X + d)
        left_here(d_core.at[0], D_X + d)
        left_here(d_f.at[0], D_Y + d)
        left_here(d_g.at[0], D_Q + d)
        left_here(u_e.at[0], U_X + d)
        left_here(u_f.at[0], U_Y + d)
        left_here(u_q.at[0], U_Q + d)
        left_here(m_q.at[0], M_Q + d)
    for hi in (0, 1):

        @pl.when(y + 4 * hi != qa)
        def _():
            left_here(d_h, D_O + hi)

    for d in range(1, 8):
        left_here(u_o.at[0], U_O + d)
        left_here(m_o.at[0], M_O + d)
    left_here(ap.at[c], A_CORE)
    left_here(u_p.at[c], U_PC)
    lay_copy.wait()


def body(tokens, base, down, up, magnitude, cotangent):
    anywhere = pl.BlockSpec(memory_space=pl.ANY)
    vmem = pl.BlockSpec(memory_space=pltpu.VMEM)
    lay, inp, mg, ug, dg = pl.pallas_call(
        kernel,
        out_shape=(
            jax.ShapeDtypeStruct((TOK, UNITS), BF16),
            jax.ShapeDtypeStruct((TOK, FEAT), BF16),
            jax.ShapeDtypeStruct((1, UNITS), F32),
            jax.ShapeDtypeStruct((RANK, UNITS), F32),
            jax.ShapeDtypeStruct((128, RANK), F32),
        ),
        in_specs=[anywhere] * 6,
        out_specs=(anywhere, anywhere, vmem, vmem, vmem),
        scratch_shapes=[
            pltpu.VMEM((TOK, FEAT), BF16),
            pltpu.VMEM((128, RANK), BF16),
            pltpu.VMEM((RANK, UNITS), BF16),
            pltpu.VMEM((1, UNITS), F32),
            pltpu.VMEM((TOK, UNITS), BF16),
            pltpu.VMEM((16, 256, UNITS), BF16),
            pltpu.VMEM((64, 128), BF16),
            pltpu.VMEM((2, 4, 16, 16, 128), BF16),
            pltpu.VMEM((16, 2, 2, 4, 16, 64), BF16),
            pltpu.VMEM((2, 1, UNITS), F32),
            pltpu.VMEM((16, 1, UNITS), F32),
            pltpu.VMEM((TOK, UNITS), BF16),
            pltpu.VMEM((TOK, RANK), BF16),
            pltpu.VMEM((TOK, UNITS), F32),
            pltpu.VMEM((TOK, UNITS), BF16),
            pltpu.VMEM((TOK, FEAT), BF16),
            pltpu.VMEM((2, 4, 16, 16, 128), F32),
            pltpu.VMEM((4, 16, 16, 128), F32),
            pltpu.VMEM((4, 16, 16, 128), F32),
            pltpu.VMEM((4, 4, 16, 128), F32),
            pltpu.VMEM((4, 4, 16, 128), F32),
            pltpu.VMEM((4, 16, 128), F32),
            pltpu.VMEM((4, 16, 128), F32),
            pltpu.VMEM((8, 16, 128), F32),
            pltpu.VMEM((16, 128), F32),
            pltpu.VMEM((4, 16, 128), F32),
            pltpu.VMEM((2, 4, 32, 128), F32),
            pltpu.VMEM((4, 32, 128), F32),
            pltpu.VMEM((4, 32, 128), F32),
            pltpu.VMEM((4, 32, 128), F32),
            pltpu.VMEM((4, 8, 128), F32),
            pltpu.VMEM((4, 8, 128), F32),
            pltpu.VMEM((8, 128), F32),
            pltpu.VMEM((4, 8, 128), F32),
            pltpu.VMEM((8, 128), F32),
            pltpu.VMEM((8, 8, 128), F32),
            pltpu.VMEM((2, 16, 8, 128), F32),
            pltpu.VMEM((2, 1, UNITS), F32),
            pltpu.VMEM((16, 1, UNITS), F32),
            pltpu.VMEM((4, 1, UNITS), F32),
            pltpu.VMEM((8, 1, UNITS), F32),
            pltpu.VMEM((1, UNITS), F32),
            pltpu.VMEM((1, UNITS), F32),
            pltpu.SemaphoreType.DMA((TOTAL,)),
            pltpu.SemaphoreType.DMA((TOTAL,)),
        ],
        compiler_params=pltpu.CompilerParams(
            collective_id=0, has_side_effects=True, vmem_limit_bytes=48 * 1024 * 1024
        ),
    )(tokens, base, down, up, magnitude.reshape(1, UNITS), cotangent)
    return lay, inp, mg.reshape(UNITS), ug, dg


def solution(mesh):
    placed = (
        P(("fsdp", "rep"), None),
        P("fsdp", None),
        P("fsdp", None),
        P(),
        P(),
        P(("fsdp", "rep"), None),
    )
    return jax.shard_map(
        body,
        mesh=mesh,
        in_specs=placed,
        out_specs=(P(("fsdp", "rep"), None), P(("fsdp", "rep"), None), P(), P(), P("fsdp", None)),
        check_vma=False,
    )
```

time: 1180 us -> 111 us (0.09)
  blocking collectives: 904 us -> 0 us
  waiting for transfers between devices: 239 us -> 0 us
  Pallas kernels: 0 us -> 100 us
  matrix products: 16.4 us -> 0 us
  between operations: 15.6 us -> 0.66 us
    psum x3 -> x0, blocking collectives: 802 us -> none  [the longest x1 443 us: body(): down_grad = lax.psum(row_sums, 'rep')]
    reduce_scatter x1 -> x0, waiting for transfers between devices: 238 us -> none  [body(): lax.psum_scatter(2.0 * factor * lax.dot_general(tokens, backward_low_rank...]
    all_gather x1 -> x0, blocking collectives: 101 us -> none  [body(): lax.all_gather(adapter_down_factor, 'fsdp', axis=0, tiled=True)]
    pallas_call x0 -> x1, Pallas kernels: none -> 100 us  [body(): pl.pallas_call(kernel, out_shape=(jax.ShapeDtypeStruct((TOK, UNITS), BF16...]
    dot_general x9 -> x0, matrix products: 16.4 us -> none  [the longest x1 4.56 us: body(): lax.dot_general(scaled_output, whole_base, (((1,), (1,)), ((), ())), pref...]
  transfers between devices with their start and end apart: 3 -> 0, of which waited for: 1 -> 0; matrix products, arithmetic and copies ran while one was open for 1% -> 0% of each run, Pallas kernels for 0% -> 0%
where the time goes in v1:
time: 111 us; the launch traced here: 110 us
  Pallas kernels  100 us (90%)
  local copies, waits for them, and re-layouts  9.34 us (8%)
    pallas_call x1, Pallas kernels, body(): pl.pallas_call(kernel, out_shape=(jax.ShapeDtypeStruct((TOK, UNITS), BF16...  100 us
    unnamed x16, local copies, waits for them, and re-layouts  9.34 us

profile of v1, /device:TPU:1, one launch (start us, length us, event | category | flops | bytes accessed | tf_op | source)
XLA Modules:
  0.0 110.1 jit_solution(11761285081884775332)
XLA Ops:
  0.6 0.8 copy.11.down_hbm
  1.5 0.0 copy-start
  1.5 1.4 %copy-done = bf16[192,4096]{1,0:T(8,128)(2,1)S(1)} copy-done((bf16[192,4096]{1,0:T(8,128)(2,1)S(1)}, bf16[192,4096]{1,0:T(8,128)(2,1)}, u32[]{:S(2)}) %copy-start) | copy-done | bytes 1572888
  2.9 0.0 copy-start.1
  2.9 0.9 copy-done.1
  3.8 0.0 copy-start.2
  3.8 0.9 copy-done.2
  4.7 0.0 copy-start.3
  4.7 0.8 copy-done.3
  5.5 0.0 copy-start.4
  5.6 0.7 copy-done.4
  6.2 100.2 %shard_map.101 = (bf16[192,512]{1,0:T(8,128)(2,1)S(1)}, bf16[192,4096]{1,0:T(8,128)(2,1)S(1)}, f32[1,512]{1,0:T(1,128)S(1)}, f32[64,512]{1,0:T(8,128)S(1)}, f32[128,64]{1,0:T(8,128)S(1)}) custom-call(bf16[192,4096]{1,0:T(8,128)(2,1)S(1)} %copy-done, bf16[128,512]{1,0:T(8,128)(2,1)S(1)} %copy-done.2, bf16[128,64]{1,0:T(8,128)(2,1)S(1)} %copy.11.down_hbm, ...), custom_call_target="tpu_custom_call" | custom-call | tf_op jit(solution)/shard_map/pallas_call | solution.py:518
  106.4 0.7 copy.12
  107.1 0.7 copy.17
  107.8 1.1 %copy.18 = bf16[192,4096]{1,0:T(8,128)(2,1)} copy(bf16[192,4096]{1,0:T(8,128)(2,1)S(1)} %get-tuple-element.26) | data formatting | bytes 3145728
  108.9 0.6 copy.19
  109.5 0.7 copy.20
Async XLA Ops:
  1.5 1.4 %copy-start = (bf16[192,4096]{1,0:T(8,128)(2,1)S(1)}, bf16[192,4096]{1,0:T(8,128)(2,1)}, u32[]{:S(2)}) copy-start(bf16[192,4096]{1,0:T(8,128)(2,1)} %tok_hbm.1) | copy-start | bytes 4718596
  2.9 0.9 copy-start.1
  3.8 0.9 copy-start.2
  4.7 0.8 copy-start.3
  5.5 0.7 copy-start.4

commit v2 on v0

v2 whole, which is shorter than its diff:
```python
import math

import jax
import jax.numpy as jnp
from jax import lax
from jax.experimental import pallas as pl
from jax.experimental.pallas import tpu as pltpu
from jax.sharding import PartitionSpec as P

MESH = pl.DeviceIdType.MESH
F32, BF16 = jnp.float32, jnp.bfloat16
TOK, FEAT, UNITS, RANK = 192, 4096, 512, 64
NT = (((1,), (1,)), ((), ()))
TN = (((0,), (0,)), ((), ()))


class Slots:
    def __init__(self):
        self.used = 0

    def take(self, count):
        base = self.used
        self.used += count
        return base


SLOTS = Slots()
LOCAL = SLOTS.take(6)
N_CORE = SLOTS.take(1)
N_Z = SLOTS.take(16)
A_Z = SLOTS.take(16)
A_X = SLOTS.take(4)
A_CORE = SLOTS.take(1)
W_Z = SLOTS.take(16)
W_X = SLOTS.take(4)
W_Y = SLOTS.take(4)
V_X = SLOTS.take(4)
V_Y = SLOTS.take(4)
W_CORE = SLOTS.take(8)
D_CORE = SLOTS.take(1)
D_P = SLOTS.take(16)
D_Q = SLOTS.take(4)
D_O = SLOTS.take(8)
D_G = SLOTS.take(16)
U_CORE = SLOTS.take(1)
U_P = SLOTS.take(16)
U_Q = SLOTS.take(4)
U_O = SLOTS.take(8)
U_G = SLOTS.take(16)
U_GC = SLOTS.take(1)
M_CORE = SLOTS.take(1)
M_P = SLOTS.take(16)
M_Q = SLOTS.take(4)
M_O = SLOTS.take(8)
OUT = SLOTS.take(17)
TOTAL = SLOTS.used


def device(x, y, z, c):
    x, y, z = lax.rem(x + 4, 4), lax.rem(y + 4, 4), lax.rem(z + 32, 32)
    return {"fsdp": lax.rem(z, 16) * 2 + c, "rep": (x * 4 + y) * 2 + z // 16}


def total8(ref):
    return ((ref[0] + ref[1]) + (ref[2] + ref[3])) + ((ref[4] + ref[5]) + (ref[6] + ref[7]))


def kernel(
    tok_hbm, base_hbm, down_hbm, up_hbm, mag_hbm, cot_hbm,
    lay_hbm, inp_hbm, mg_ref, ug_ref, dg_ref,
    tok, own_w, own_a, b_ref, mag, cot,
    wn, wf, ap,
    n_core, n_z,
    scaled_ref, back_ref, lin, lay, inp,
    d_all, d_core, d_half, d_p, d_s, d_q, d_h, d_o, d_g,
    u_all, u_core, u_e, u_p, u_q, u_o, u_g,
    m_core, m_p, m_q, m_o,
    ss, rs,
):
    f_at, r_at = lax.axis_index("fsdp"), lax.axis_index("rep")
    c, zl = lax.rem(f_at, 2), f_at // 2
    zh, xy = lax.rem(r_at, 2), r_at // 2
    x, y, z = xy // 4, lax.rem(xy, 4), zh * 16 + zl
    qb, qa = lax.rem(z, 4), z // 4
    sib = device(x, y, z, 1 - c)
    factor = 1.0 / math.sqrt(196608.0)

    def remote(src, dst, s, r, to):
        return pltpu.make_async_remote_copy(
            src_ref=src, dst_ref=dst, send_sem=ss.at[s], recv_sem=rs.at[r],
            device_id=to, device_id_type=MESH,
        )

    def arrived(dst, r):
        remote(dst, dst, r, r, sib).wait_recv()

    def left_here(src, s):
        remote(src, src, s, s, sib).wait_send()

    def plane(i):
        return lax.rem(x + i // 4, 4), lax.rem(y + lax.rem(i, 4), 4)

    def loop(first, last, step):
        def one(i, _):
            step(i)
            return 0

        lax.fori_loop(first, last, one, 0)

    barrier = pltpu.get_barrier_semaphore()
    near = (-1, 1, -2, 2, -3, 3, -4, 4, -5, 5, -6, 6, -7, 7, -8, 8)
    peers = [device(x, y, z + d, c) for d in near]
    peers += [device(x + i, y + j, z, c) for i in range(4) for j in range(4) if i or j]
    peers += [sib]
    for peer in peers:
        pl.semaphore_signal(barrier, 1, device_id=peer, device_id_type=MESH)

    loads = [
        pltpu.make_async_copy(base_hbm, own_w, rs.at[LOCAL]),
        pltpu.make_async_copy(down_hbm, own_a, rs.at[LOCAL + 1]),
        pltpu.make_async_copy(up_hbm, b_ref, rs.at[LOCAL + 2]),
        pltpu.make_async_copy(mag_hbm, mag, rs.at[LOCAL + 3]),
        pltpu.make_async_copy(cot_hbm, cot, rs.at[LOCAL + 4]),
        pltpu.make_async_copy(tok_hbm, tok, rs.at[LOCAL + 5]),
    ]
    for load in loads:
        load.start()

    loads[0].wait()
    loads[1].wait()
    loads[2].wait()
    merged = own_w[...].astype(F32) + 2.0 * lax.dot_general(
        own_a[...], b_ref[...], TN, preferred_element_type=F32
    )
    n_core[c] = jnp.sum(merged * merged, axis=0, keepdims=True)
    rows_y = pl.ds(pl.multiple_of(y * 32, 32), 32)
    lanes_x = pl.ds(pl.multiple_of(x * 128, 128), 128)
    wn[c, y, x, 4] = own_w[rows_y, lanes_x]
    ap[c, x, zl] = own_a[pl.ds(pl.multiple_of(x * 16, 16), 16), :]
    pl.semaphore_wait(barrier, len(peers))

    n_copy = remote(n_core.at[c], n_core.at[c], N_CORE, N_CORE, sib)
    n_copy.start()
    w_piece = wn.at[c, y, x, 4]

    def w_near(d):
        remote(w_piece, wn.at[c, y, x, 4 - d], W_Z + (4 - d), W_Z + (4 - d), device(x, y, z + d, c)).start()

    def w_far(j):
        d = jnp.where(j < 12, 4 - j, 20 - j)
        remote(w_piece, wf.at[c, x, y, j - 8], W_Z + j, W_Z + j, device(x, y, z + d, c)).start()

    for d in (1, -1, 2, -2, 3, -3, 4):
        w_near(d)
    n_copy.wait()
    n_z[zl] = n_core[0] + n_core[1]

    def z_offset(i):
        return jnp.where(lax.rem(i, 2) == 0, i // 2 + 1, -(i // 2) - 1)

    def n_send(i):
        remote(n_z.at[zl], n_z.at[zl], N_Z + i, N_Z + zl, device(x, y, z + z_offset(i), c)).start()

    loop(0, 15, n_send)
    loop(8, 16, w_far)

    def a_send(i):
        part = ap.at[c, x, zl]
        remote(part, part, A_Z + i, A_Z + zl, device(x, y, z + z_offset(i), c)).start()

    loop(0, 15, a_send)

    for j in (0, 1, 2, 3, 5, 6, 7):
        arrived(wn.at[c, y, x, j], W_Z + j)
    for d in (1, 2, 3):
        part = wn.at[c, y, x]
        remote(part, part, W_X + d, W_X + d, device(x + d, y, z, c)).start()

    def n_wait(i):
        slot = lax.rem(zl - z_offset(i) + 16, 16)
        arrived(n_z.at[slot], N_Z + slot)

    loop(0, 15, n_wait)
    loads[3].wait()
    loads[4].wait()
    squares = jnp.sum(n_z[...], axis=0)
    col_norm = jnp.sqrt(squares + 1e-06)
    scaling = mag[...] / col_norm
    scaled = (cot[...].astype(F32) * scaling).astype(BF16)
    scaled_ref[...] = scaled
    back = lax.dot_general(scaled, b_ref[...], NT, preferred_element_type=F32).astype(BF16)
    back_ref[...] = back
    back_t = (back.astype(F32).T).astype(BF16)
    loads[5].wait()

    def d_part(k_at):
        for n in range(4):
            part = (2.0 * factor) * jnp.dot(
                back_t, tok[:, n * 1024 : n * 1024 + 1024], preferred_element_type=F32
            )
            for r in range(4):
                for k in range(2):
                    at = r * 256 + k * 128
                    d_all[k, :, n, r] = part[:, at : at + 128].reshape(4, 16, 128)

    d_part(0)
    d_core_copy = remote(d_all.at[1 - c], d_core, D_CORE, D_CORE, sib)
    d_core_copy.start()

    for j in range(8, 16):
        arrived(wf.at[c, x, y, j - 8], W_Z + j)
    for d in (1, 2, 3):
        part = wf.at[c, x, y]
        remote(part, part, V_Y + d, V_Y + d, device(x, y + d, z, c)).start()

    def around(at, d):
        return lax.rem(at + d + 4, 4)

    def block_send(buf, at, base_sem, core_sem, ahead, behind):
        block = buf.at[c, at]
        remote(block, block, base_sem, base_sem, ahead).start()
        remote(block, block, base_sem + 1, base_sem + 1, behind).start()
        remote(block, block, core_sem, core_sem, sib).start()

    def block_forward(buf, at, base_sem, core_sem, ahead, behind):
        before, after = around(at, -1), around(at, 1)
        arrived(buf.at[c, before], base_sem)
        half = buf.at[c, before, 0:2]
        remote(half, half, base_sem + 2, base_sem + 2, ahead).start()
        arrived(buf.at[c, after], base_sem + 1)
        half = buf.at[c, after, 2:4]
        remote(half, half, base_sem + 3, base_sem + 3, behind).start()
        remote(buf.at[c, before], buf.at[c, before], core_sem + 1, core_sem + 1, sib).start()
        remote(buf.at[c, after], buf.at[c, after], core_sem + 2, core_sem + 2, sib).start()

    def block_last(buf, at, base_sem, core_sem):
        last = around(at, 2)
        arrived(buf.at[c, last, 0:2], base_sem + 2)
        arrived(buf.at[c, last, 2:4], base_sem + 3)
        remote(buf.at[c, last], buf.at[c, last], core_sem + 3, core_sem + 3, sib).start()

    def block_core(buf, at, core_sem):
        for n, d in enumerate((0, -1, 1, 2)):
            arrived(buf.at[1 - c, around(at, d)], core_sem + n)

    def block_sent(buf, at, base_sem, core_sem):
        left_here(buf.at[c, at], base_sem)
        left_here(buf.at[c, at], base_sem + 1)
        left_here(buf.at[c, at, 0:2], base_sem + 2)
        left_here(buf.at[c, at, 2:4], base_sem + 3)
        for n in range(4):
            left_here(buf.at[c, at], core_sem + n)

    near_y = (wn, y, W_Y, W_CORE)
    far_x = (wf, x, V_X, W_CORE + 4)
    y_ahead, y_behind = device(x, y + 1, z, c), device(x, y - 1, z, c)
    x_ahead, x_behind = device(x + 1, y, z, c), device(x - 1, y, z, c)

    for d in (1, 2, 3):
        arrived(wn.at[c, y, lax.rem(x - d + 4, 4)], W_X + d)
    block_send(*near_y, y_ahead, y_behind)

    d_core_copy.wait()
    for i in range(4):
        d_half[i] = (d_core[i] + d_all[c, i]).astype(BF16)

    def d_send(i):
        px, py = plane(i)
        remote(d_half.at[px, py], d_p.at[xy], D_P + i, D_P + xy, device(px, py, z, c)).start()

    loop(1, 16, d_send)
    d_p[xy] = d_half[x, y]

    def a_wait(i):
        slot = lax.rem(zl - z_offset(i) + 16, 16)
        arrived(ap.at[c, x, slot], A_Z + slot)

    loop(0, 15, a_wait)
    for d in (1, 2, 3):
        remote(ap.at[c, x], ap.at[c, x], A_X + d, A_X + d, device(x + d, y, z, c)).start()

    for d in (1, 2, 3):
        arrived(wf.at[c, x, lax.rem(y - d + 4, 4)], V_Y + d)
    block_send(*far_x, x_ahead, x_behind)
    block_forward(*near_y, y_ahead, y_behind)

    for d in (1, 2, 3):
        arrived(ap.at[c, lax.rem(x - d + 4, 4)], A_X + d)
    a_core_copy = remote(ap.at[c], ap.at[c], A_CORE, A_CORE, sib)
    a_core_copy.start()

    def d_wait(i):
        px, py = plane(i)
        arrived(d_p.at[px * 4 + py], D_P + px * 4 + py)

    loop(1, 16, d_wait)
    for r in range(4):
        d_s[r] = jnp.sum(d_p[:, r].astype(F32), axis=0)
    for d in (1, 2, 3):
        to = lax.rem(qb + d, 4)
        remote(d_s.at[to], d_q.at[qb], D_Q + d, D_Q + d, device(x, y, qa * 4 + to, c)).start()
    d_q[qb] = d_s[qb]

    block_forward(*far_x, x_ahead, x_behind)

    def columns(res):
        return pl.ds(pl.multiple_of(res * 256, 256), 256)

    def a_pair(res):
        return jnp.concatenate([ap[0, :, res].reshape(64, 128), ap[1, :, res].reshape(64, 128)], axis=1)

    arrived(ap.at[1 - c], A_CORE)
    low_sum = jnp.zeros((TOK, RANK), F32)
    for n in range(4):
        a_four = jnp.concatenate([a_pair(n * 4 + r) for r in range(4)], axis=1)
        low_sum = low_sum + lax.dot_general(
            tok[:, n * 1024 : n * 1024 + 1024], a_four, NT, preferred_element_type=F32
        )
    low = low_sum.astype(BF16)
    up_part = (2.0 * factor) * lax.dot_general(low, scaled_ref[...], TN, preferred_element_type=F32)
    for k in range(2):
        for q in range(4):
            u_all[k, q] = up_part[k * 32 : k * 32 + 32, q * 128 : q * 128 + 128].reshape(4, 8, 128)
    u_core_copy = remote(u_all.at[1 - c], u_core, U_CORE, U_CORE, sib)
    u_core_copy.start()
    lin[...] = 2.0 * jnp.dot(low, b_ref[...], preferred_element_type=F32)

    block_last(*near_y)

    owner = lax.rem(qa, 4) == y
    for d in (1, 2, 3):
        arrived(d_q.at[lax.rem(qb - d + 4, 4)], D_Q + d)
    d_h[...] = (d_q[0] + d_q[1]) + (d_q[2] + d_q[3])
    for hi in (0, 1):
        to = y + 4 * hi

        @pl.when(to != qa)
        def _():
            remote(d_h, d_o.at[qa], D_O + hi, D_O + qa, device(x, y, to * 4 + qb, c)).start()

    u_core_copy.wait()
    u_e[...] = u_all[c] + u_core[...]

    def u_send(i):
        px, py = plane(i)
        remote(u_e.at[px, py], u_p.at[xy], U_P + i, U_P + xy, device(px, py, z, c)).start()

    loop(1, 16, u_send)
    u_p[xy] = u_e[x, y]

    block_last(*far_x)

    def near_pair(j):
        return jnp.concatenate([wn[:, :, q, j].reshape(256, 128) for q in range(4)], axis=1)

    def far_pair(j):
        return jnp.concatenate([wf[:, q, :, j].reshape(256, 128) for q in range(4)], axis=1)

    def near_at(j):
        return lax.rem(zl + j + 12, 16)

    def far_at(j):
        return lax.rem(zl + j + 20, 16)

    def forward(pair, at):
        def two(i):
            j = i * 2
            first = jnp.dot(tok[:, columns(at(j))], pair(j), preferred_element_type=F32)
            second = jnp.dot(tok[:, columns(at(j + 1))], pair(j + 1), preferred_element_type=F32)
            lin[...] += first + second

        loop(0, 4, two)

    def backward(pair, at, first, last):
        def one(j):
            res = at(j)
            grad = lax.dot_general(scaled_ref[...], pair(j), NT, preferred_element_type=F32)
            grad = grad + 2.0 * jnp.dot(back_ref[...], a_pair(res), preferred_element_type=F32)
            inp[:, columns(res)] = grad.astype(BF16)
            pltpu.make_async_copy(
                inp.at[:, columns(res)], inp_hbm.at[:, columns(res)], rs.at[OUT + res]
            ).start()

        loop(first, last, one)

    block_core(wn, y, W_CORE)
    forward(near_pair, near_at)

    def u_wait(i):
        px, py = plane(i)
        arrived(u_p.at[px * 4 + py], U_P + px * 4 + py)

    loop(1, 16, u_wait)
    u_q[qb] = jnp.sum(u_p[...], axis=0)
    for d in (1, 2, 3):
        to = lax.rem(qb + d, 4)
        remote(u_q.at[qb], u_q.at[qb], U_Q + d, U_Q + d, device(x, y, qa * 4 + to, c)).start()

    block_core(wf, x, W_CORE + 4)
    forward(far_pair, far_at)

    m_core[c] = jnp.sum(cot[...].astype(F32) * lin[...], axis=0, keepdims=True)
    m_core_copy = remote(m_core.at[c], m_core.at[c], M_CORE, M_CORE, sib)
    m_core_copy.start()
    backward(near_pair, near_at, 0, 4)
    m_core_copy.wait()
    m_p[xy] = m_core[0] + m_core[1]

    def m_send(i):
        px, py = plane(i)
        remote(m_p.at[xy], m_p.at[xy], M_P + i, M_P + xy, device(px, py, z, c)).start()

    loop(1, 16, m_send)

    for d in (1, 2, 3):
        arrived(u_q.at[lax.rem(qb - d + 4, 4)], U_Q + d)
    u_o[qa] = (u_q[0] + u_q[1]) + (u_q[2] + u_q[3])
    for d in range(1, 8):
        to = lax.rem(qa + d, 8)
        remote(u_o.at[qa], u_o.at[qa], U_O + d, U_O + d, device(x, y, to * 4 + qb, c)).start()

    backward(near_pair, near_at, 4, 8)

    @pl.when(owner)
    def _():
        d_o[qa] = d_h[...]
        for d in range(1, 8):
            at = lax.rem(qa - d + 8, 8)
            arrived(d_o.at[at], D_O + at)
        d_g[x] = total8(d_o)

        def g_send(i):
            px, py = plane(i)
            remote(d_g.at[x], d_g.at[x], D_G + i, D_G + x, device(px, py, z, c)).start()

        loop(1, 16, g_send)

    def m_wait(i):
        px, py = plane(i)
        arrived(m_p.at[px * 4 + py], M_P + px * 4 + py)

    loop(1, 16, m_wait)
    m_q[qb] = jnp.sum(m_p[...], axis=0)
    for d in (1, 2, 3):
        to = lax.rem(qb + d, 4)
        remote(m_q.at[qb], m_q.at[qb], M_Q + d, M_Q + d, device(x, y, qa * 4 + to, c)).start()
    lay[...] = (lin[...] * scaling).astype(BF16)
    lay_copy = pltpu.make_async_copy(lay, lay_hbm, rs.at[OUT + 16])
    lay_copy.start()
    backward(far_pair, far_at, 0, 3)
    for d in (1, 2, 3):
        arrived(m_q.at[lax.rem(qb - d + 4, 4)], M_Q + d)
    m_o[qa] = (m_q[0] + m_q[1]) + (m_q[2] + m_q[3])
    for d in range(1, 8):
        to = lax.rem(qa + d, 8)
        remote(m_o.at[qa], m_o.at[qa], M_O + d, M_O + d, device(x, y, to * 4 + qb, c)).start()

    for d in range(1, 8):
        arrived(u_o.at[lax.rem(qa - d + 8, 8)], U_O + d)
    u_g[c, xy] = total8(u_o)

    def ug_send(i):
        px, py = plane(i)
        part = u_g.at[c, xy]
        remote(part, part, U_G + i, U_G + xy, device(px, py, z, c)).start()

    loop(1, 16, ug_send)

    backward(far_pair, far_at, 3, 8)

    def ug_wait(i):
        px, py = plane(i)
        arrived(u_g.at[c, px * 4 + py], U_G + px * 4 + py)

    loop(1, 16, ug_wait)
    ug_copy = remote(u_g.at[c], u_g.at[c], U_GC, U_GC, sib)
    ug_copy.start()

    def dg_wait(i):
        @pl.when(jnp.logical_or(i != x, jnp.logical_not(owner)))
        def _():
            arrived(d_g.at[i], D_G + i)

    loop(0, 4, dg_wait)
    dg_ref[...] = d_g[...].reshape(64, 128)
    ug_copy.wait()
    for k in range(2):
        for q in range(4):
            ug_ref[k * 32 : k * 32 + 32, q * 128 : q * 128 + 128] = u_g[
                k, q * 4 : q * 4 + 4
            ].reshape(32, 128)

    def sent(i):
        left_here(n_z.at[zl], N_Z + i)
        left_here(ap.at[c, x, zl], A_Z + i)
        left_here(d_p.at[0], D_P + i + 1)
        left_here(u_p.at[0], U_P + i + 1)
        left_here(m_p.at[xy], M_P + i + 1)
        left_here(u_g.at[c, xy], U_G + i + 1)

        @pl.when(owner)
        def _():
            left_here(d_g.at[x], D_G + i + 1)

    loop(0, 15, sent)
    for j in (0, 1, 2, 3, *range(5, 16)):
        left_here(w_piece, W_Z + j)
    for d in (1, 2, 3):
        left_here(ap.at[c, x], A_X + d)
        left_here(wn.at[c, y, x], W_X + d)
        left_here(wf.at[c, x, y], V_Y + d)
        left_here(d_s.at[0], D_Q + d)
        left_here(u_q.at[0], U_Q + d)
        left_here(m_q.at[0], M_Q + d)
    for hi in (0, 1):

        @pl.when(y + 4 * hi != qa)
        def _():
            left_here(d_h, D_O + hi)

    for d in range(1, 8):
        left_here(u_o.at[0], U_O + d)
        left_here(m_o.at[0], M_O + d)
    left_here(ap.at[c], A_CORE)
    block_sent(*near_y)
    block_sent(*far_x)
    lay_copy.wait()

    def stored(i):
        pltpu.make_async_copy(
            inp.at[:, columns(i)], inp_hbm.at[:, columns(i)], rs.at[OUT + i]
        ).wait()

    loop(0, 16, stored)

    for d in range(1, 8):
        arrived(m_o.at[lax.rem(qa - d + 8, 8)], M_O + d)
    mg_ref[...] = total8(m_o) / col_norm * factor


def hand_over(*refs):
    sources, targets, held, came, went = refs[:5], refs[5:10], refs[10:15], refs[15], refs[16]
    parts = []
    for i in (1, 0, 3, 4, 2):
        rows = sources[i].shape[0]
        step = 48 if i == 1 else rows
        for first in range(0, rows, step):
            at = pl.ds(first, step)
            parts.append((sources[i].at[at], held[i].at[at], targets[i].at[at]))
    into = [pltpu.make_async_copy(p[0], p[1], came.at[n]) for n, p in enumerate(parts)]
    out = [pltpu.make_async_copy(p[1], p[2], went.at[n]) for n, p in enumerate(parts)]
    for copy in into:
        copy.start()
    for first, second in zip(into, out):
        first.wait()
        second.start()
    for copy in out:
        copy.wait()


def body(tokens, base, down, up, magnitude, cotangent):
    anywhere = pl.BlockSpec(memory_space=pl.ANY)
    vmem = pl.BlockSpec(memory_space=pltpu.VMEM)
    shapes = (
        jax.ShapeDtypeStruct((TOK, UNITS), BF16),
        jax.ShapeDtypeStruct((TOK, FEAT), BF16),
        jax.ShapeDtypeStruct((1, UNITS), F32),
        jax.ShapeDtypeStruct((RANK, UNITS), F32),
        jax.ShapeDtypeStruct((RANK, 128), F32),
    )
    results = pl.pallas_call(
        kernel,
        out_shape=shapes,
        in_specs=[anywhere] * 6,
        out_specs=(anywhere, anywhere, vmem, vmem, vmem),
        scratch_shapes=[
            pltpu.VMEM((TOK, FEAT), BF16),
            pltpu.VMEM((128, UNITS), BF16),
            pltpu.VMEM((RANK, 128), BF16),
            pltpu.VMEM((RANK, UNITS), BF16),
            pltpu.VMEM((1, UNITS), F32),
            pltpu.VMEM((TOK, UNITS), BF16),
            pltpu.VMEM((2, 4, 4, 8, 32, 128), BF16),
            pltpu.VMEM((2, 4, 4, 8, 32, 128), BF16),
            pltpu.VMEM((2, 4, 16, 16, 128), BF16),
            pltpu.VMEM((2, 1, UNITS), F32),
            pltpu.VMEM((16, 1, UNITS), F32),
            pltpu.VMEM((TOK, UNITS), BF16),
            pltpu.VMEM((TOK, RANK), BF16),
            pltpu.VMEM((TOK, UNITS), F32),
            pltpu.VMEM((TOK, UNITS), BF16),
            pltpu.VMEM((TOK, FEAT), BF16),
            pltpu.VMEM((2, 4, 4, 4, 16, 128), F32),
            pltpu.VMEM((4, 4, 4, 16, 128), F32),
            pltpu.VMEM((4, 4, 4, 16, 128), BF16),
            pltpu.VMEM((16, 4, 16, 128), BF16),
            pltpu.VMEM((4, 16, 128), F32),
            pltpu.VMEM((4, 16, 128), F32),
            pltpu.VMEM((16, 128), F32),
            pltpu.VMEM((8, 16, 128), F32),
            pltpu.VMEM((4, 16, 128), F32),
            pltpu.VMEM((2, 4, 4, 8, 128), F32),
            pltpu.VMEM((4, 4, 8, 128), F32),
            pltpu.VMEM((4, 4, 8, 128), F32),
            pltpu.VMEM((16, 8, 128), F32),
            pltpu.VMEM((4, 8, 128), F32),
            pltpu.VMEM((8, 8, 128), F32),
            pltpu.VMEM((2, 16, 8, 128), F32),
            pltpu.VMEM((2, 1, UNITS), F32),
            pltpu.VMEM((16, 1, UNITS), F32),
            pltpu.VMEM((4, 1, UNITS), F32),
            pltpu.VMEM((8, 1, UNITS), F32),
            pltpu.SemaphoreType.DMA((TOTAL,)),
            pltpu.SemaphoreType.DMA((TOTAL,)),
        ],
        compiler_params=pltpu.CompilerParams(
            collective_id=0, has_side_effects=True, vmem_limit_bytes=60 * 1024 * 1024
        ),
    )(tokens, base, down.T, up, magnitude.reshape(1, UNITS), cotangent)
    lay, inp, mg, ug, dg = pl.pallas_call(
        hand_over,
        out_shape=shapes,
        in_specs=[anywhere] * 5,
        out_specs=(anywhere,) * 5,
        scratch_shapes=[pltpu.VMEM(shape.shape, shape.dtype) for shape in shapes]
        + [pltpu.SemaphoreType.DMA((8,)), pltpu.SemaphoreType.DMA((8,))],
        compiler_params=pltpu.CompilerParams(vmem_limit_bytes=60 * 1024 * 1024),
    )(*results)
    return lay, inp, mg.reshape(UNITS), ug, dg.T


def solution(mesh):
    placed = (
        P(("fsdp", "rep"), None),
        P("fsdp", None),
        P("fsdp", None),
        P(),
        P(),
        P(("fsdp", "rep"), None),
    )
    return jax.shard_map(
        body,
        mesh=mesh,
        in_specs=placed,
        out_specs=(P(("fsdp", "rep"), None), P(("fsdp", "rep"), None), P(), P(), P("fsdp", None)),
        check_vma=False,
    )
```

time: 1180 us -> 92.1 us (0.08)
  blocking collectives: 904 us -> 0 us
  waiting for transfers between devices: 239 us -> 0 us
  Pallas kernels: 0 us -> 91.3 us
  matrix products: 16.4 us -> 0 us
  between operations: 15.6 us -> 0.64 us
    psum x3 -> x0, blocking collectives: 802 us -> none  [the longest x1 443 us: body(): down_grad = lax.psum(row_sums, 'rep')]
    reduce_scatter x1 -> x0, waiting for transfers between devices: 238 us -> none  [body(): lax.psum_scatter(2.0 * factor * lax.dot_general(tokens, backward_low_rank...]
    all_gather x1 -> x0, blocking collectives: 101 us -> none  [body(): lax.all_gather(adapter_down_factor, 'fsdp', axis=0, tiled=True)]
    pallas_call x0 -> x2, Pallas kernels: none -> 91.3 us  [the longest x1 88.9 us: body(): pl.pallas_call(kernel, out_shape=shapes, in_specs=[anywhere] * 6, out_spe...]
    dot_general x9 -> x0, matrix products: 16.4 us -> none  [the longest x1 4.56 us: body(): lax.dot_general(scaled_output, whole_base, (((1,), (1,)), ((), ())), pref...]
  transfers between devices with their start and end apart: 3 -> 0, of which waited for: 1 -> 0; matrix products, arithmetic and copies ran while one was open for 1% -> 0% of each run, Pallas kernels for 0% -> 0%
where the time goes in v2:
time: 92.1 us; the launch traced here: 91.9 us
  Pallas kernels  91.3 us (99%)
    pallas_call x1, Pallas kernels, body(): pl.pallas_call(kernel, out_shape=shapes, in_specs=[anywhere] * 6, out_spe...  88.9 us
    pallas_call x1, Pallas kernels, body(): pl.pallas_call(hand_over, out_shape=shapes, in_specs=[anywhere] * 5, out_...  2.38 us

profile of v2, /device:TPU:1, one launch (start us, length us, event | category | flops | bytes accessed | tf_op | source)
XLA Modules:
  0.0 91.9 jit_solution(7241069370600546904)
XLA Ops:
  0.6 88.9 %shard_map.101 = (bf16[192,512]{1,0:T(8,128)(2,1)}, bf16[192,4096]{1,0:T(8,128)(2,1)}, f32[1,512]{1,0:T(1,128)}, f32[64,512]{1,0:T(8,128)}, f32[64,128]{1,0:T(8,128)}) custom-call(bf16[192,4096]{1,0:T(8,128)(2,1)} %tok_hbm.1, bf16[128,512]{1,0:T(8,128)(2,1)} %base_hbm.1, bf16[64,128]{1,0:T(8,128)(2,1)} %bitcast.4, bf16[64,512]{1,0:T(8,128)(2,1)} %up_hbm.1, ...), custom_call_target="tpu_custom_call" | custom-call | tf_op jit(solution)/shard_map/pallas_call | solution.py:571
  89.5 2.4 %shard_map.102 = (bf16[192,512]{1,0:T(8,128)(2,1)}, bf16[192,4096]{1,0:T(8,128)(2,1)}, f32[1,512]{1,0:T(1,128)}, f32[64,512]{1,0:T(8,128)}, f32[64,128]{1,0:T(8,128)}) custom-call(bf16[192,512]{1,0:T(8,128)(2,1)} %get-tuple-element.15.refs_0_, bf16[192,4096]{1,0:T(8,128)(2,1)} %get-tuple-element.16.refs_1_, f32[1,512]{1,0:T(1,128)} %get-tuple-element.17.refs_2_, ...), custom_call_target="tpu_custom_call" | custom-call | tf_op jit(solution)/shard_map/pallas_call | solution.py:620

commit v3 on v2

--- a/solution.py
+++ b/solution.py
@@ -37,6 +37,10 @@
 V_X = SLOTS.take(4)
 V_Y = SLOTS.take(4)
 W_CORE = SLOTS.take(8)
+W_PA = SLOTS.take(4)
+W_PB = SLOTS.take(4)
+V_PA = SLOTS.take(4)
+V_PB = SLOTS.take(4)
 D_CORE = SLOTS.take(1)
 D_P = SLOTS.take(16)
 D_Q = SLOTS.take(4)
@@ -150,6 +154,19 @@
         d = jnp.where(j < 12, 4 - j, 20 - j)
         remote(w_piece, wf.at[c, x, y, j - 8], W_Z + j, W_Z + j, device(x, y, z + d, c)).start()
 
+    y_ahead, y_behind = device(x, y + 1, z, c), device(x, y - 1, z, c)
+    x_ahead, x_behind = device(x + 1, y, z, c), device(x - 1, y, z, c)
+
+    def near_piece(p):
+        part = wn.at[c, y, p]
+        remote(part, part, W_PA + p, W_PA + p, y_ahead).start()
+        remote(part, part, W_PB + p, W_PB + p, y_behind).start()
+
+    def far_piece(p):
+        part = wf.at[c, x, p]
+        remote(part, part, V_PA + p, V_PA + p, x_ahead).start()
+        remote(part, part, V_PB + p, V_PB + p, x_behind).start()
+
     for d in (1, -1, 2, -2, 3, -3, 4):
         w_near(d)
     n_copy.wait()
@@ -175,6 +192,7 @@
     for d in (1, 2, 3):
         part = wn.at[c, y, x]
         remote(part, part, W_X + d, W_X + d, device(x + d, y, z, c)).start()
+    near_piece(x)
 
     def n_wait(i):
         slot = lax.rem(zl - z_offset(i) + 16, 16)
@@ -212,24 +230,28 @@
     for d in (1, 2, 3):
         part = wf.at[c, x, y]
         remote(part, part, V_Y + d, V_Y + d, device(x, y + d, z, c)).start()
+    far_piece(y)
 
     def around(at, d):
         return lax.rem(at + d + 4, 4)
 
-    def block_send(buf, at, base_sem, core_sem, ahead, behind):
+    def block_send(buf, at, core_sem):
         block = buf.at[c, at]
-        remote(block, block, base_sem, base_sem, ahead).start()
-        remote(block, block, base_sem + 1, base_sem + 1, behind).start()
         remote(block, block, core_sem, core_sem, sib).start()
 
-    def block_forward(buf, at, base_sem, core_sem, ahead, behind):
+    def block_forward(buf, at, base_sem, core_sem, pa, pb, ahead, behind):
         before, after = around(at, -1), around(at, 1)
-        arrived(buf.at[c, before], base_sem)
+        for p in range(2):
+            arrived(buf.at[c, before, p], pa + p)
         half = buf.at[c, before, 0:2]
         remote(half, half, base_sem + 2, base_sem + 2, ahead).start()
-        arrived(buf.at[c, after], base_sem + 1)
+        for p in range(2, 4):
+            arrived(buf.at[c, after, p], pb + p)
         half = buf.at[c, after, 2:4]
         remote(half, half, base_sem + 3, base_sem + 3, behind).start()
+        for p in range(2):
+            arrived(buf.at[c, before, 2 + p], pa + (2 + p))
+            arrived(buf.at[c, after, p], pb + p)
         remote(buf.at[c, before], buf.at[c, before], core_sem + 1, core_sem + 1, sib).start()
         remote(buf.at[c, after], buf.at[c, after], core_sem + 2, core_sem + 2, sib).start()
 
@@ -243,9 +265,10 @@
         for n, d in enumerate((0, -1, 1, 2)):
             arrived(buf.at[1 - c, around(at, d)], core_sem + n)
 
-    def block_sent(buf, at, base_sem, core_sem):
-        left_here(buf.at[c, at], base_sem)
-        left_here(buf.at[c, at], base_sem + 1)
+    def block_sent(buf, at, base_sem, core_sem, pa, pb):
+        for p in range(4):
+            left_here(buf.at[c, at, p], pa + p)
+            left_here(buf.at[c, at, p], pb + p)
         left_here(buf.at[c, at, 0:2], base_sem + 2)
         left_here(buf.at[c, at, 2:4], base_sem + 3)
         for n in range(4):
@@ -253,12 +276,10 @@
 
     near_y = (wn, y, W_Y, W_CORE)
     far_x = (wf, x, V_X, W_CORE + 4)
-    y_ahead, y_behind = device(x, y + 1, z, c), device(x, y - 1, z, c)
-    x_ahead, x_behind = device(x + 1, y, z, c), device(x - 1, y, z, c)
-
-    for d in (1, 2, 3):
-        arrived(wn.at[c, y, lax.rem(x - d + 4, 4)], W_X + d)
-    block_send(*near_y, y_ahead, y_behind)
+    for d in (1, 3, 2):
+        arrived(wn.at[c, y, around(x, -d)], W_X + d)
+        near_piece(around(x, -d))
+    block_send(wn, y, W_CORE)
 
     d_core_copy.wait()
     for i in range(4):
@@ -279,10 +300,11 @@
     for d in (1, 2, 3):
         remote(ap.at[c, x], ap.at[c, x], A_X + d, A_X + d, device(x + d, y, z, c)).start()
 
-    for d in (1, 2, 3):
-        arrived(wf.at[c, x, lax.rem(y - d + 4, 4)], V_Y + d)
-    block_send(*far_x, x_ahead, x_behind)
-    block_forward(*near_y, y_ahead, y_behind)
+    for d in (1, 3, 2):
+        arrived(wf.at[c, x, around(y, -d)], V_Y + d)
+        far_piece(around(y, -d))
+    block_send(wf, x, W_CORE + 4)
+    block_forward(*near_y, W_PA, W_PB, y_ahead, y_behind)
 
     for d in (1, 2, 3):
         arrived(ap.at[c, lax.rem(x - d + 4, 4)], A_X + d)
@@ -301,7 +323,7 @@
         remote(d_s.at[to], d_q.at[qb], D_Q + d, D_Q + d, device(x, y, qa * 4 + to, c)).start()
     d_q[qb] = d_s[qb]
 
-    block_forward(*far_x, x_ahead, x_behind)
+    block_forward(*far_x, V_PA, V_PB, x_ahead, x_behind)
 
     def columns(res):
         return pl.ds(pl.multiple_of(res * 256, 256), 256)
@@ -522,8 +544,8 @@
         left_here(u_o.at[0], U_O + d)
         left_here(m_o.at[0], M_O + d)
     left_here(ap.at[c], A_CORE)
-    block_sent(*near_y)
-    block_sent(*far_x)
+    block_sent(*near_y, W_PA, W_PB)
+    block_sent(*far_x, V_PA, V_PB)
     lay_copy.wait()
 
     def stored(i):

time: 92.1 us -> 91.2 us (level)
    pallas_call x1, Pallas kernels: 88.9 us -> 88 us  [body(): pl.pallas_call(kernel, out_shape=shapes, in_specs=[anywhere] * 6, out_spe...]
where the time goes in v3:
time: 91.2 us; the launch traced here: 91 us
  Pallas kernels  90.4 us (99%)
    pallas_call x1, Pallas kernels, body(): pl.pallas_call(kernel, out_shape=shapes, in_specs=[anywhere] * 6, out_spe...  88 us
    pallas_call x1, Pallas kernels, body(): pl.pallas_call(hand_over, out_shape=shapes, in_specs=[anywhere] * 5, out_...  2.38 us

profile of v3, /device:TPU:1, one launch (start us, length us, event | category | flops | bytes accessed | tf_op | source)
XLA Modules:
  0.0 91.0 jit_solution(5764978033858146355)
XLA Ops:
  0.6 88.0 %shard_map.101 = (bf16[192,512]{1,0:T(8,128)(2,1)}, bf16[192,4096]{1,0:T(8,128)(2,1)}, f32[1,512]{1,0:T(1,128)}, f32[64,512]{1,0:T(8,128)}, f32[64,128]{1,0:T(8,128)}) custom-call(bf16[192,4096]{1,0:T(8,128)(2,1)} %tok_hbm.1, bf16[128,512]{1,0:T(8,128)(2,1)} %base_hbm.1, bf16[64,128]{1,0:T(8,128)(2,1)} %bitcast.4, bf16[64,512]{1,0:T(8,128)(2,1)} %up_hbm.1, ...), custom_call_target="tpu_custom_call" | custom-call | tf_op jit(solution)/shard_map/pallas_call | solution.py:593
  88.6 2.4 %shard_map.102 = (bf16[192,512]{1,0:T(8,128)(2,1)}, bf16[192,4096]{1,0:T(8,128)(2,1)}, f32[1,512]{1,0:T(1,128)}, f32[64,512]{1,0:T(8,128)}, f32[64,128]{1,0:T(8,128)}) custom-call(bf16[192,512]{1,0:T(8,128)(2,1)} %get-tuple-element.15.refs_0_, bf16[192,4096]{1,0:T(8,128)(2,1)} %get-tuple-element.16.refs_1_, f32[1,512]{1,0:T(1,128)} %get-tuple-element.17.refs_2_, ...), custom_call_target="tpu_custom_call" | custom-call | tf_op jit(solution)/shard_map/pallas_call | solution.py:642
